TPU v7x, 512 devices: a whole 4x4x16 slice. The times are simulated.
512 devices in a mesh: snp: 32 (over y, x, core), samp: 16 (over z).
Axes of the slice: x: 4, y: 4, z: 16, core: 2. Of those that a mesh axis runs over, the one named last changes fastest.
Arguments:
- dosages: bfloat16 [24576, 16384], P('samp', 'snp'), may hold values from 0 to 2
- observed: int32 [24576, 16384], P('samp', 'snp'), may hold values from 0 to 1, as said below
Outputs:
- band_gram: float32 [16384, 1536], P(('snp', 'samp'))
Inputs may be any that keep to these rules, and one draw needn't show every extreme that they name: Some SNP columns are missing in every sample, so their count of observed samples is 0.
All inputs are finite; a program needn't handle non-finite values.
Results may differ from a plain program's by a relative error of at most 0.00095.
Values may be sent and summed in bfloat16 or wider, within the bound.
A program may use at most 64 MiB of HBM per device.

v0:
```python
import jax
import jax.numpy as jnp
from jax import lax
from jax.sharding import PartitionSpec as P


def shifted(block, axis, distance):
    devices = range(lax.axis_size(axis))
    route = [(i - distance, i) for i in devices if i - distance in devices]
    return lax.ppermute(block, axis, route)


def cross_rows(left, right, scale):
    gram = lax.dot_general(
        left, right, (((0,), (0,)), ((), ())), preferred_element_type=jnp.float32
    )
    return gram * scale


def local(dosages, observed):
    mask_f = observed.astype(jnp.float32)
    values = dosages.astype(jnp.float32)
    count, total, squares = lax.psum(
        (
            jnp.sum(mask_f, axis=0),
            jnp.sum(mask_f * values, axis=0),
            jnp.sum(mask_f * values * values, axis=0),
        ),
        "samp",
    )
    count = jnp.maximum(count, 1.0)
    mean = total / count
    var = squares / count - mean * mean
    standard = (mask_f * (values - mean) * lax.rsqrt(var + 1e-05)).astype(jnp.bfloat16)
    scale = 1.0 / (dosages.shape[0] * lax.axis_size("samp"))
    following = shifted(standard, "snp", -1)
    further = shifted(standard, "snp", -2)
    wide = jnp.concatenate([standard, following, further], axis=1)
    return lax.psum_scatter(
        cross_rows(standard, wide, scale), "samp", scatter_dimension=0, tiled=True
    )


def solution(mesh):
    return jax.shard_map(
        local,
        mesh=mesh,
        in_specs=(P("samp", "snp"), P("samp", "snp")),
        out_specs=P(("snp", "samp"), None),
        check_vma=False,
    )
```

profile of v0, /device:TPU:10, one launch (start us, length us, event | category | flops | bytes accessed | tf_op | source)
XLA Modules:
  0.0 182.2 jit_solution(15910102067035268098)
XLA Ops:
  6.5 0.0 copy-start
  6.5 0.0 reduce-scatter.2.cloned.1.call-start
  6.5 3.3 %fusion.13 = (f32[512]{0:T(512)S(1)}, f32[512]{0:T(512)S(1)}, f32[512]{0:T(512)S(1)}) fusion(bf16[1536,512]{1,0:T(8,128)(2,1)} %param.2, s32[1536,512]{1,0:T(8,128)} %param.3), kind=kLoop, calls=%fused_computation.15 | loop fusion | flops 5503488 | bytes 4724736 | tf_op jit(solution)/shard_map/reduce_sum | solution.py:26
  9.8 37.0 %all-reduce = (f32[512]{0:T(512)S(1)}, f32[512]{0:T(512)S(1)}, f32[512]{0:T(512)S(1)}) all-reduce(f32[512]{0:T(512)S(1)} %get-tuple-element.6, f32[512]{0:T(512)S(1)} %get-tuple-element.7, f32[512]{0:T(512)S(1)} %get-tuple-element.5), channel_id=1, replica_groups=mesh['snp'=32,'samp'=16] {'samp'}, use_global_device_ids=true, to_apply=%region_5.0 | all-reduce | flops 1536 | bytes 12288 | tf_op jit(solution)/shard_map/psum | solution.py:23
  46.8 0.0 copy-done
  46.9 2.0 %fusion.8 = bf16[1536,512]{1,0:T(8,128)(2,1)S(1)} fusion(bf16[1536,512]{1,0:T(8,128)(2,1)} %param.2, s32[1536,512]{1,0:T(8,128)S(1)} %copy-done, f32[512]{0:T(512)S(1)} %get-tuple-element.12, f32[512]{0:T(512)S(1)} %get-tuple-element.11), kind=kLoop, calls=%fused_computation.11 | loop fusion | flops 4718592 | bytes 6295552 | tf_op jit(solution)/shard_map/convert_element_type | solution.py:34
  48.9 2.4 %collective-permute-start.1 = (bf16[1536,512]{1,0:T(8,128)(2,1)S(1)}, bf16[1536,512]{1,0:T(8,128)(2,1)S(1)}, u32[]{:S(2)}, u32[]{:S(2)}) collective-permute-start(bf16[1536,512]{1,0:T(8,128)(2,1)S(1)} %fusion.8), channel_id=1, source_target_pairs={{32,0},{48,16},{64,32},{80,48},{96,64},{112,80},{128,96},{144,112}... | collective-permute-start | bytes 4718600 | tf_op jit(solution)/shard_map/ppermute | solution.py:10
  51.3 1.9 %collective-permute-start = (bf16[1536,512]{1,0:T(8,128)(2,1)S(1)}, bf16[1536,512]{1,0:T(8,128)(2,1)S(1)}, u32[]{:S(2)}, u32[]{:S(2)}) collective-permute-start(bf16[1536,512]{1,0:T(8,128)(2,1)S(1)} %fusion.8), channel_id=1, source_target_pairs={{16,0},{32,16},{48,32},{64,48},{80,64},{96,80},{112,96},{128,112},... | collective-permute-start | bytes 4718600 | tf_op jit(solution)/shard_map/ppermute | solution.py:10
  53.3 26.6 %collective-permute-done.1 = bf16[1536,512]{1,0:T(8,128)(2,1)S(1)} collective-permute-done((bf16[1536,512]{1,0:T(8,128)(2,1)S(1)}, bf16[1536,512]{1,0:T(8,128)(2,1)S(1)}, u32[]{:S(2)}, u32[]{:S(2)}) %collective-permute-start.1) | collective-permute-done | bytes 1572896 | tf_op jit(solution)/shard_map/ppermute | solution.py:10
  79.9 14.9 %collective-permute-done = bf16[1536,512]{1,0:T(8,128)(2,1)S(1)} collective-permute-done((bf16[1536,512]{1,0:T(8,128)(2,1)S(1)}, bf16[1536,512]{1,0:T(8,128)(2,1)S(1)}, u32[]{:S(2)}, u32[]{:S(2)}) %collective-permute-start) | collective-permute-done | bytes 1572896 | tf_op jit(solution)/shard_map/ppermute | solution.py:10
  94.8 4.5 %fusion.10 = f32[512,1536]{1,0:T(8,128)} fusion(bf16[1536,512]{1,0:T(8,128)(2,1)S(1)} %fusion.8, bf16[1536,512]{1,0:T(8,128)(2,1)S(1)} %collective-permute-done.1, bf16[1536,512]{1,0:T(8,128)(2,1)S(1)} %collective-permute-done), kind=kOutput, calls=%fused_computation.14 | convolution fusion | flops 2430861312 | bytes 7864320 | tf_op jit(solution)/shard_map/dot_general | solution.py:14
  99.3 0.0 reduce-scatter.2.cloned.1.call-update
  99.3 76.1 %reduce-scatter.2.cloned.1.call-done = f32[32,1536]{1,0:T(8,128)} async-done(((f32[512,1536]{1,0:T(8,128)}), f32[32,1536]{1,0:T(8,128)}) %reduce-scatter.2.cloned.1.call-update) | async-done | bytes 196624 | tf_op jit(solution)/shard_map/reduce_scatter | solution.py:39
  (1 shorter events, 0.0 us)
Async XLA Ops:
  6.5 40.3 %copy-start = (s32[1536,512]{1,0:T(8,128)S(1)}, s32[1536,512]{1,0:T(8,128)}, u32[]{:S(2)}) copy-start(s32[1536,512]{1,0:T(8,128)} %param.3) | copy-start | bytes 9437188
  6.5 168.8 %reduce-scatter.2.cloned.1.call-start = ((), (), s32[]{:S(2)}) async-start(), calls=%async_computation.1 | async-start | bytes 3342336 | tf_op jit(solution)/shard_map/reduce_scatter | solution.py:39
  48.9 31.0 %collective-permute-start.1 = (bf16[1536,512]{1,0:T(8,128)(2,1)S(1)}, bf16[1536,512]{1,0:T(8,128)(2,1)S(1)}, u32[]{:S(2)}, u32[]{:S(2)}) collective-permute-start(bf16[1536,512]{1,0:T(8,128)(2,1)S(1)} %fusion.8), channel_id=1, source_target_pairs={{32,0},{48,16},{64,32},{80,48},{96,64},{112,80},{128,96},{144,112}... | collective-permute-start | bytes 4718600 | tf_op jit(solution)/shard_map/ppermute | solution.py:10
  51.3 43.4 %collective-permute-start = (bf16[1536,512]{1,0:T(8,128)(2,1)S(1)}, bf16[1536,512]{1,0:T(8,128)(2,1)S(1)}, u32[]{:S(2)}, u32[]{:S(2)}) collective-permute-start(bf16[1536,512]{1,0:T(8,128)(2,1)S(1)} %fusion.8), channel_id=1, source_target_pairs={{16,0},{32,16},{48,32},{64,48},{80,64},{96,80},{112,96},{128,112},... | collective-permute-start | bytes 4718600 | tf_op jit(solution)/shard_map/ppermute | solution.py:10
Sparse Core Ops, SparseCore 0:
  99.4 75.8 reduce-scatter.1
where the time goes:
time: 182 us
  waiting for transfers between devices  118 us (65%)
  blocking collectives  37 us (20%)
  between operations  13.4 us (7%)
  other arithmetic  5.33 us (3%)
  matrix products  4.49 us (2%)
  starting transfers between devices  4.37 us (2%)
    reduce_scatter x1, waiting for transfers between devices, local(): lax.psum_scatter(cross_rows(standard, wide, scale), 'samp', scatter_dimen...  76.1 us
    ppermute x2, waiting for transfers between devices, shifted(): return lax.ppermute(block, axis, route)  41.5 us
    psum x1, blocking collectives, local(): lax.psum((jnp.sum(mask_f, axis=0), jnp.sum(mask_f * values, axis=0), jnp....  37 us
    dot_general x1, matrix products, cross_rows(): lax.dot_general(left, right, (((0,), (0,)), ((), ())), preferred_element_...  4.49 us
    ppermute x2, starting transfers between devices, shifted(): return lax.ppermute(block, axis, route)  4.36 us
  transfers between devices with their start and end apart: 3, of which 3 were waited for; matrix products, arithmetic and copies ran while one was open for 0% of the time, Pallas kernels for 0%

commit v1 on v0

v1 whole, which is shorter than its diff:
```python
import functools
import math

import jax
import jax.numpy as jnp
from jax import lax
from jax.experimental import pallas as pl
from jax.experimental.pallas import tpu as pltpu
from jax.sharding import PartitionSpec as P

MESH = pl.DeviceIdType.MESH
F32 = jnp.float32
BF16 = jnp.bfloat16

STEPS = 1650.0
FINE = 4096.0


def encode(x):
    q = jnp.minimum(STEPS * jnp.log(1.0 + FINE * jnp.abs(x)) + 0.5, 32767.0).astype(
        jnp.int32
    )
    return jnp.where(x < 0.0, -q, q).astype(jnp.int16)


def decode(q):
    f = q.astype(jnp.int32).astype(F32)
    a = (jnp.exp(jnp.abs(f) * (1.0 / STEPS)) - 1.0) * (1.0 / FINE)
    return jnp.where(f < 0.0, -a, a)


def gram(left, right):
    return lax.dot_general(
        left, right, (((0,), (0,)), ((), ())), preferred_element_type=F32
    )


class Chain:
    def __init__(self, groups, stride, part, stage, slots, send, recv, device):
        self.groups, self.stride = groups, stride
        self.reach = (groups // 2, groups - 1 - groups // 2)
        self.part, self.stage, self.slots = part, stage, slots
        self.send, self.recv, self.device = send, recv, device

    def hop(self, way, offset, source, number):
        stride, reach = self.stride, self.reach[way]
        length = min(stride, offset)
        slot = offset - stride if offset > stride else reach - stride + offset
        sign = 1 if way == 0 else -1
        return pltpu.make_async_remote_copy(
            src_ref=source,
            dst_ref=self.slots.at[way, slot - 1],
            send_sem=self.send.at[way, number],
            recv_sem=self.recv.at[way, slot - 1],
            device_id=self.device(sign * length),
            device_id_type=MESH,
        )

    def arrival(self, way, slot):
        ref = self.slots.at[way, slot - 1]
        return pltpu.make_async_copy(ref, ref, self.recv.at[way, slot - 1])

    def own(self, way, offset):
        me = lax.axis_index("samp")
        sign = 1 if way == 0 else -1
        return lax.rem(me + sign * offset + self.groups, self.groups)

    def source(self, way, offset):
        reach, stride = self.reach[way], self.stride
        if offset + stride > reach:
            return self.stage.at[way, reach - offset]
        return self.slots.at[way, offset - 1]

    def visit(self, way, offset):
        reach, stride = self.reach[way], self.stride
        ref = self.source(way, offset)
        total = self.part[self.own(way, offset)]
        if offset + stride <= reach:
            self.arrival(way, offset).wait()
            total = total + decode(ref[...])
        ref[...] = encode(total)
        self.hop(way, offset, ref, offset - 1).start()

    def start(self):
        for way in (0, 1):
            for offset in range(self.reach[way], self.reach[way] - self.stride, -1):
                self.visit(way, offset)

    def levels(self):
        top = self.reach[0] - self.stride
        steps = []
        while top > 0:
            steps.append(
                [
                    (way, offset)
                    for offset in range(top, max(top - self.stride, 0), -1)
                    for way in (0, 1)
                    if offset + self.stride <= self.reach[way]
                ]
            )
            top -= self.stride
        return steps

    def finish(self):
        total = self.part[lax.axis_index("samp")]
        for way in (0, 1):
            for near in range(1, self.stride + 1):
                slot = self.reach[way] - self.stride + near
                self.arrival(way, slot).wait()
                total = total + decode(self.slots[way, slot - 1])
        return total

    def drain(self):
        for way in (0, 1):
            for offset in range(1, self.reach[way] + 1):
                self.hop(way, offset, self.source(way, offset), offset - 1).wait_send()


def band_kernel(
    groups,
    chips,
    dosages,
    observed,
    out,
    dose_v,
    seen_v,
    stats,
    blocks,
    ordered,
    ahead,
    behind,
    part_e,
    part_l,
    stage_e,
    stage_l,
    slots_e,
    slots_l,
    give_e,
    give_l,
    give_p,
    take_e,
    take_l,
    take_p,
    load_sem,
    stat_send,
    stat_recv,
    core_send,
    core_recv,
    x_send,
    x_recv,
    e_send,
    e_recv,
    l_send,
    l_recv,
    f_send,
    f_recv,
):
    snp, me = lax.axis_index("snp"), lax.axis_index("samp")
    core = lax.rem(snp, 2)
    chip = lax.div(snp, 2)
    rows, width = dose_v.shape
    samples = rows * groups
    count_snp = 2 * chips

    def along(distance):
        return (snp, lax.rem(me + distance + groups, groups))

    other = (snp + 1 - 2 * core, me)
    before = (lax.rem(snp + count_snp - 2, count_snp), me)
    after = (lax.rem(snp + 2, count_snp), me)
    cross = (lax.rem(snp + count_snp + 2 * core - 1, count_snp), me)
    before_b = (lax.rem(2 * chip + count_snp - 1, count_snp), me)

    def remote(src, dst, send, recv, device):
        return pltpu.make_async_remote_copy(
            src_ref=src,
            dst_ref=dst,
            send_sem=send,
            recv_sem=recv,
            device_id=device,
            device_id_type=MESH,
        )

    pieces = load_sem.shape[1]
    high = rows // pieces

    def load(piece):
        span = pl.ds(piece * high, high)
        return (
            pltpu.make_async_copy(
                dosages.at[span], dose_v.at[span], load_sem.at[0, piece]
            ),
            pltpu.make_async_copy(
                observed.at[span], seen_v.at[span], load_sem.at[1, piece]
            ),
        )

    for piece in range(pieces):
        for copy in load(piece):
            copy.start()

    barrier = pltpu.get_barrier_semaphore()
    peers = [along(d) for d in range(1, groups)] + [other, before, after, cross]
    for peer in peers:
        pl.semaphore_signal(barrier, inc=1, device_id=peer, device_id_type=MESH)

    def add_rows(step, carry):
        span = pl.ds(pl.multiple_of(step * 32, 32), 32)
        v = dose_v[span].astype(F32)
        m = seen_v[span].astype(F32)
        mv = m * v
        sums = []
        for acc, term in zip(carry, (m, mv, mv * v)):
            sums.append(acc + jnp.sum(term.reshape(4, 8, width), axis=0))
        return tuple(sums)

    carry = tuple(jnp.zeros((8, width), F32) for _ in range(3))
    for piece in range(pieces):
        for copy in load(piece):
            copy.wait()
        carry = lax.fori_loop(
            piece * high // 32, (piece + 1) * high // 32, add_rows, carry
        )
    lanes = width // 128
    stats[me] = jnp.zeros(stats.shape[1:], F32)
    for kind, acc in enumerate(carry):
        line = jnp.sum(acc, axis=0, keepdims=True)
        for lane in range(lanes):
            row = kind * lanes + lane
            stats[me, row : row + 1, :] = line[:, lane * 128 : lane * 128 + 128]

    pl.semaphore_wait(barrier, len(peers))

    half = groups // 2
    order = [half] + [sign * d for d in range(half - 1, 0, -1) for sign in (1, -1)]
    posts = []
    for number, distance in enumerate(order):
        posts.append(
            remote(
                stats.at[me],
                stats.at[me],
                stat_send.at[number],
                stat_recv.at[lax.rem(distance + groups, groups)],
                along(distance),
            )
        )
        posts[-1].start()
    for distance in range(1, groups):
        origin = lax.rem(me - distance + groups, groups)
        ref = stats.at[origin]
        pltpu.make_async_copy(ref, ref, stat_recv.at[distance]).wait()
    total = stats[0]
    for group in range(1, groups):
        total = total + stats[group]
    count = jnp.maximum(total[0:lanes], 1.0)
    mean = total[lanes : 2 * lanes] / count
    var = total[2 * lanes : 3 * lanes] / count - mean * mean
    rate = lax.rsqrt(var + 1e-05)
    mean_line = jnp.concatenate([mean[i : i + 1] for i in range(lanes)], axis=1)
    rate_line = jnp.concatenate([rate[i : i + 1] for i in range(lanes)], axis=1)

    def standardize(step, carry):
        span = pl.ds(pl.multiple_of(step * 32, 32), 32)
        v = dose_v[span].astype(F32)
        m = seen_v[span].astype(F32)
        blocks[core, span, :] = (m * (v - mean_line) * rate_line).astype(BF16)
        return carry

    lax.fori_loop(0, rows // 32, standardize, 0)

    swap = remote(
        blocks.at[core], blocks.at[core], core_send.at[0], core_recv.at[0], other
    )
    swap.start()

    def ahead_copy(chunk):
        cols = pl.ds(pl.multiple_of(core * 256 + chunk * 128, 128), 128)
        return remote(
            blocks.at[0, :, cols],
            ahead.at[chunk],
            x_send.at[0, chunk],
            x_recv.at[0, chunk],
            before,
        )

    def behind_copy(chunk):
        return remote(
            ordered.at[chunk],
            behind.at[chunk],
            x_send.at[1, chunk],
            x_recv.at[1, chunk],
            after,
        )

    def send_ahead():
        for chunk in range(2):
            ahead_copy(chunk).start()

    def send_behind():
        for chunk in range(2):
            line = lax.broadcasted_iota(jnp.int32, (width, 128), 0)
            col = lax.broadcasted_iota(jnp.int32, (width, 128), 1)
            from_row = 32 * (col // 8) + 16 * core + 8 * chunk + lax.rem(col, 8)
            pick = jnp.where(line == from_row, 1.0, 0.0).astype(BF16)
            ordered[chunk] = jnp.dot(
                blocks[1], pick, preferred_element_type=F32
            ).astype(BF16)
            behind_copy(chunk).start()

    pl.when(core == 0)(send_ahead)
    pl.when(core == 1)(send_behind)

    early = Chain(groups, 1, part_e, stage_e, slots_e, e_send, e_recv, along)
    late = [
        Chain(
            groups,
            2,
            part_l.at[chunk],
            stage_l.at[chunk],
            slots_l.at[chunk],
            l_send.at[chunk],
            l_recv.at[chunk],
            along,
        )
        for chunk in range(2)
    ]

    for strip in range(4):
        cols = slice(strip * 128, strip * 128 + 128)
        product = gram(blocks[core, :, cols], blocks[core])
        part_e[strip * 4 : strip * 4 + 4, :, 0:512] = product.reshape(4, 32, 512)

    swap.wait()
    pl.when(core == 1)(send_ahead)
    pl.when(core == 0)(send_behind)

    half_cols = pl.ds(pl.multiple_of(core * 256, 256), 256)
    product = gram(blocks[0], blocks[1, :, half_cols])
    part_e[:, :, 512:768] = product.reshape(16, 32, 256)

    early.start()

    def late_gram(chunk):
        ahead_copy(chunk).wait()
        behind_copy(chunk).wait()
        part = part_l.at[chunk]
        for block in range(2):
            product = gram(blocks[block], ahead[chunk])
            part[:, :, block * 128 : block * 128 + 128] = product.reshape(16, 32, 128)
        product = gram(behind[chunk], blocks[1])
        for piece in range(4):
            cols = slice(piece * 128, piece * 128 + 128)
            part[:, piece * 8 : piece * 8 + 8, 256:384] = product[:, cols].reshape(
                16, 8, 128
            )
        late[chunk].start()

    scale = 1.0 / samples
    last = chip == chips - 1

    def level(chain, number):
        for way, offset in chain.levels()[number]:
            chain.visit(way, offset)

    for number in range(3):
        level(early, number)
    late_gram(0)
    for number in range(3, 5):
        level(early, number)
    level(late[0], 0)
    late_gram(1)
    for number in range(5, 7):
        level(early, number)
        level(late[0], number - 4)
    level(late[1], 0)

    total = early.finish() * scale
    out[:, 0:512] = total[:, 0:512]
    give_e[...] = total[:, 512:768]

    def early_copy():
        return remote(give_e, take_e, f_send.at[0], f_recv.at[0], other)

    pl.when(core == 1)(lambda: early_copy().start())

    def put_early():
        out[:, 512:768] = give_e[...]

    pl.when(core == 0)(put_early)

    def late_copy(chunk):
        return remote(
            give_l.at[chunk],
            take_l.at[chunk],
            f_send.at[1 + chunk],
            f_recv.at[1 + chunk],
            other,
        )

    def back_copy(chunk):
        return remote(
            give_p.at[chunk],
            take_p.at[core, chunk],
            f_send.at[3 + chunk],
            f_recv.at[3 + 2 * core + chunk],
            before_b,
        )

    def late_end(chunk):
        total = late[chunk].finish() * scale
        give_p[chunk] = total[:, 256:384]
        back_copy(chunk).start()
        first = jnp.where(last, 0.0, total[:, 0:128])
        second = jnp.where(last, 0.0, total[:, 128:256])
        give_l[chunk] = jnp.where(core == 0, second, first)
        late_copy(chunk).start()

        def first_core():
            out[:, 1024 + 128 * chunk : 1152 + 128 * chunk] = first

        def second_core():
            out[:, 768 + 128 * chunk : 896 + 128 * chunk] = second

        pl.when(core == 0)(first_core)
        pl.when(core == 1)(second_core)

    late_end(0)
    for number in range(1, 3):
        level(late[1], number)
    late_end(1)

    def arrived(ref, sem):
        pltpu.make_async_copy(ref, ref, sem).wait()

    def first_core_end():
        arrived(take_e, f_recv.at[0])
        out[:, 768:1024] = take_e[...]
        for chunk in range(2):
            arrived(take_l.at[chunk], f_recv.at[1 + chunk])
            out[:, 1280 + 128 * chunk : 1408 + 128 * chunk] = take_l[chunk]

    def second_core_end():
        for chunk in range(2):
            arrived(take_l.at[chunk], f_recv.at[1 + chunk])
            out[:, 512 + 128 * chunk : 640 + 128 * chunk] = take_l[chunk]
        for side in range(2):
            for chunk in range(2):
                ref = take_p.at[side, chunk]
                arrived(ref, f_recv.at[3 + 2 * side + chunk])
                value = jnp.where(last, 0.0, ref[...])
                for piece in range(4):
                    out[
                        16 * side + 8 * chunk : 16 * side + 8 * chunk + 8,
                        1024 + 128 * piece : 1152 + 128 * piece,
                    ] = value[piece * 8 : piece * 8 + 8]

    pl.when(core == 0)(first_core_end)
    pl.when(core == 1)(second_core_end)

    for post in posts:
        post.wait_send()
    early.drain()
    for chunk in range(2):
        late[chunk].drain()
        late_copy(chunk).wait_send()
        back_copy(chunk).wait_send()
    pl.when(core == 1)(lambda: early_copy().wait_send())


def solution(mesh):
    groups, snps = mesh.shape["samp"], mesh.shape["snp"]

    def local(dosages, observed):
        rows, width = dosages.shape
        vmem = pltpu.VMEM
        dma = pltpu.SemaphoreType.DMA
        return pl.pallas_call(
            functools.partial(band_kernel, groups, snps // 2),
            out_shape=jax.ShapeDtypeStruct((width // groups, 3 * width), F32),
            in_specs=[pl.BlockSpec(memory_space=pl.ANY)] * 2,
            out_specs=pl.BlockSpec(memory_space=pltpu.VMEM),
            scratch_shapes=[
                vmem((rows, width), BF16),
                vmem((rows, width), jnp.int32),
                vmem((groups, 16, 128), F32),
                vmem((2, rows, width), BF16),
                vmem((2, rows, 128), BF16),
                vmem((2, rows, 128), BF16),
                vmem((2, rows, 128), BF16),
                vmem((groups, 32, 768), F32),
                vmem((2, groups, 32, 384), F32),
                vmem((2, 1, 32, 768), jnp.int16),
                vmem((2, 2, 2, 32, 384), jnp.int16),
                vmem((2, 8, 32, 768), jnp.int16),
                vmem((2, 2, 8, 32, 384), jnp.int16),
                vmem((32, 256), F32),
                vmem((2, 32, 128), F32),
                vmem((2, 32, 128), F32),
                vmem((32, 256), F32),
                vmem((2, 32, 128), F32),
                vmem((2, 2, 32, 128), F32),
                dma((2, 6)),
                dma((groups,)),
                dma((groups,)),
                dma((1,)),
                dma((1,)),
                dma((2, 2)),
                dma((2, 2)),
                dma((2, 8)),
                dma((2, 8)),
                dma((2, 2, 8)),
                dma((2, 2, 8)),
                dma((5,)),
                dma((7,)),
            ],
            compiler_params=pltpu.CompilerParams(
                collective_id=0,
                has_side_effects=True,
                vmem_limit_bytes=56 * 2**20,
            ),
            cost_estimate=pl.CostEstimate(
                flops=2 * 3 * rows * width * width,
                bytes_accessed=6 * rows * width,
                transcendentals=0,
            ),
            name="band",
        )(dosages, observed)

    return jax.shard_map(
        local,
        mesh=mesh,
        in_specs=(P("samp", "snp"), P("samp", "snp")),
        out_specs=P(("snp", "samp"), None),
        check_vma=False,
    )
```

time: 182 us -> 80.4 us (0.44)
  the two profiles are of different devices: /device:TPU:10 before, /device:TPU:1 now
where the time goes in v1:
time: 80.4 us; the launch traced here: 80.2 us
  Pallas kernels  78.6 us (98%)
  local copies, waits for them, and re-layouts  1.62 us (2%)
    pallas_call x1, Pallas kernels, local(): pl.pallas_call(functools.partial(band_kernel, groups, snps // 2), out_sha...  78.6 us
    unnamed x1, local copies, waits for them, and re-layouts  1.62 us

profile of v1, /device:TPU:1, one launch (start us, length us, event | category | flops | bytes accessed | tf_op | source)
XLA Modules:
  0.0 80.2 jit_solution(15892775254250962658)
XLA Ops:
  0.0 78.6 %band.1 = f32[32,1536]{1,0:T(8,128)} custom-call(bf16[1536,512]{1,0:T(8,128)(2,1)} %dosages.1, s32[1536,512]{1,0:T(8,128)} %observed.1), custom_call_target="tpu_custom_call" | custom-call | flops 2415919104 | bytes 4718592 | tf_op jit(solution)/shard_map/band/pallas_call | solution.py:477
  78.6 1.6 %copy.4 = f32[32,1536]{1,0:T(8,128)} copy(f32[32,1536]{1,0:T(8,128)} %band.1) | data formatting | bytes 393216

commit v2 on v1

v2 whole, which is shorter than its diff:
```python
import functools
import math

import jax
import jax.numpy as jnp
from jax import lax
from jax.experimental import pallas as pl
from jax.experimental.pallas import tpu as pltpu
from jax.sharding import PartitionSpec as P

MESH = pl.DeviceIdType.MESH
F32 = jnp.float32
BF16 = jnp.bfloat16

STEPS = 1650.0
FINE = 4096.0


STRIDES = (1, 1, 1, 1, 1, 2)
ORDER = (((0, 0), (0, 1), (0, 2), (0, 3), (0, 4), (0, 5), (0, 6), (0, 7), (0, 8),), ((0, 0), (0, 1), (1, 0), (2, 0), (3, 0), (1, 1), (0, 2), (2, 1), (4, 0), (3, 1), (1, 2), (0, 3), (2, 2), (4, 1), (3, 2), (1, 3), (5, 0), (4, 2), (2, 3), (0, 4), (3, 3), (1, 4), (4, 3), (2, 4), (0, 5), (3, 4), (5, 1), (1, 5), (4, 4), (2, 5), (0, 6), (3, 5), (1, 6), (4, 5), (2, 6), (5, 2), (0, 7), (3, 6), (1, 7), (4, 6), (2, 7), (0, 8), (3, 7), (5, 3), (1, 8), (4, 7), (2, 8), (3, 8), (5, 4), (4, 8),))


def encode(x):
    q = jnp.minimum(STEPS * jnp.log(1.0 + FINE * jnp.abs(x)) + 0.5, 32767.0).astype(
        jnp.int32
    )
    return jnp.where(x < 0.0, -q, q).astype(jnp.int16)


def decode(q):
    f = q.astype(jnp.int32).astype(F32)
    a = (jnp.exp(jnp.abs(f) * (1.0 / STEPS)) - 1.0) * (1.0 / FINE)
    return jnp.where(f < 0.0, -a, a)


def gram(left, right):
    return lax.dot_general(
        left, right, (((0,), (0,)), ((), ())), preferred_element_type=F32
    )


class Chain:
    def __init__(self, groups, stride, part, stage, slots, send, recv, device):
        self.groups = groups
        self.reach = (groups // 2, groups - 1 - groups // 2)
        self.stride = tuple(min(stride, reach) for reach in self.reach)
        self.part, self.stage, self.slots = part, stage, slots
        self.send, self.recv, self.device = send, recv, device

    def hop(self, way, offset, source, number):
        stride, reach = self.stride[way], self.reach[way]
        length = min(stride, offset)
        slot = offset - stride if offset > stride else reach - stride + offset
        sign = 1 if way == 0 else -1
        return pltpu.make_async_remote_copy(
            src_ref=source,
            dst_ref=self.slots.at[way, slot - 1],
            send_sem=self.send.at[way, number],
            recv_sem=self.recv.at[way, slot - 1],
            device_id=self.device(sign * length),
            device_id_type=MESH,
        )

    def arrival(self, way, slot):
        ref = self.slots.at[way, slot - 1]
        return pltpu.make_async_copy(ref, ref, self.recv.at[way, slot - 1])

    def own(self, way, offset):
        me = lax.axis_index("samp")
        sign = 1 if way == 0 else -1
        return lax.rem(me + sign * offset + self.groups, self.groups)

    def source(self, way, offset):
        reach, stride = self.reach[way], self.stride[way]
        if offset + stride > reach:
            return self.stage.at[way, reach - offset]
        return self.slots.at[way, offset - 1]

    def visit(self, way, offset):
        reach, stride = self.reach[way], self.stride[way]
        ref = self.source(way, offset)
        total = self.part[self.own(way, offset)]
        if offset + stride <= reach:
            self.arrival(way, offset).wait()
            total = total + decode(ref[...])
        ref[...] = encode(total)
        self.hop(way, offset, ref, offset - 1).start()

    def levels(self):
        steps = []
        for way in (0, 1):
            for place, offset in enumerate(range(self.reach[way], 0, -1)):
                number = place // self.stride[way]
                if number == len(steps):
                    steps.append([])
                steps[number].append((place, way, offset))
        return [[visit[1:] for visit in sorted(step)] for step in steps]

    def finish(self):
        total = self.part[lax.axis_index("samp")]
        for near in range(1, max(self.stride) + 1):
            for way in (0, 1):
                if near > self.stride[way]:
                    continue
                slot = self.reach[way] - self.stride[way] + near
                self.arrival(way, slot).wait()
                total = total + decode(self.slots[way, slot - 1])
        return total

    def drain(self):
        for way in (0, 1):
            for offset in range(1, self.reach[way] + 1):
                self.hop(way, offset, self.source(way, offset), offset - 1).wait_send()


def band_kernel(
    groups,
    chips,
    dosages,
    observed,
    out,
    dose_v,
    seen_v,
    stats,
    blocks,
    picks,
    ordered,
    ahead,
    behind,
    raw_ours,
    raw_ahead,
    raw_behind,
    line_ours,
    line_ahead,
    line_behind,
    part_e,
    part_l,
    stage_e,
    stage_l,
    slots_e,
    slots_l,
    give_e,
    give_l,
    give_p,
    take_e,
    take_l,
    take_p,
    load_sem,
    stat_send,
    stat_recv,
    core_send,
    core_recv,
    x_send,
    x_recv,
    r_send,
    r_recv,
    e_send,
    e_recv,
    l_send,
    l_recv,
    f_send,
    f_recv,
):
    snp, me = lax.axis_index("snp"), lax.axis_index("samp")
    core = lax.rem(snp, 2)
    chip = lax.div(snp, 2)
    rows, width = dose_v.shape
    samples = rows * groups
    count_snp = 2 * chips

    def along(distance):
        return (snp, lax.rem(me + distance + groups, groups))

    other = (snp + 1 - 2 * core, me)
    before_b = (lax.rem(2 * chip + count_snp - 1, count_snp), me)
    after_b = (lax.rem(2 * chip + 3, count_snp), me)
    after_a = (lax.rem(2 * chip + 2, count_snp), me)

    def remote(src, dst, send, recv, device):
        return pltpu.make_async_remote_copy(
            src_ref=src,
            dst_ref=dst,
            send_sem=send,
            recv_sem=recv,
            device_id=device,
            device_id_type=MESH,
        )

    pieces = load_sem.shape[1]
    high = rows // pieces

    def load(piece):
        span = pl.ds(piece * high, high)
        return (
            pltpu.make_async_copy(
                dosages.at[span], dose_v.at[span], load_sem.at[0, piece]
            ),
            pltpu.make_async_copy(
                observed.at[span], seen_v.at[span], load_sem.at[1, piece]
            ),
        )

    for piece in range(pieces):
        for copy in load(piece):
            copy.start()

    def make_picks():
        line = lax.broadcasted_iota(jnp.int32, (width, width), 0)
        col = lax.broadcasted_iota(jnp.int32, (width, width), 1)
        from_row = 32 * ((col >> 3) & 15) + 8 * (col >> 7) + (col & 7)
        picks[...] = jnp.where(line == from_row, 1.0, 0.0).astype(BF16)

    barrier = pltpu.get_barrier_semaphore()

    def greet(peers):
        for peer in peers:
            pl.semaphore_signal(barrier, inc=1, device_id=peer, device_id_type=MESH)

    greet([along(d) for d in range(1, groups)] + [other, before_b])
    pl.when(core == 1)(lambda: greet([after_a, after_b]))

    def add_rows(step, carry):
        span = pl.ds(pl.multiple_of(step * 32, 32), 32)
        v = dose_v[span].astype(F32)
        m = seen_v[span].astype(F32)
        mv = m * v
        sums = []
        for acc, term in zip(carry, (m, mv, mv * v)):
            sums.append(acc + jnp.sum(term.reshape(4, 8, width), axis=0))
        return tuple(sums)

    carry = tuple(jnp.zeros((8, width), F32) for _ in range(3))
    for piece in range(pieces):
        for copy in load(piece):
            copy.wait()
        carry = lax.fori_loop(
            piece * high // 32, (piece + 1) * high // 32, add_rows, carry
        )
    lanes = width // 128
    stats[me] = jnp.zeros(stats.shape[1:], F32)
    for kind, acc in enumerate(carry):
        line = jnp.sum(acc, axis=0, keepdims=True)
        for lane in range(lanes):
            row = kind * lanes + lane
            stats[me, row : row + 1, :] = line[:, lane * 128 : lane * 128 + 128]

    def raw_first():
        raw_ours[0] = dose_v[:, 0:128]
        raw_ours[1] = seen_v[:, 0:128].astype(F32).astype(BF16)

    def raw_second():
        make_picks()
        pick = picks[:, 0:128]
        raw_ours[0] = jnp.dot(
            dose_v[...], pick, preferred_element_type=F32
        ).astype(BF16)
        raw_ours[1] = jnp.dot(
            seen_v[...].astype(F32).astype(BF16), pick, preferred_element_type=F32
        ).astype(BF16)

    def raw_copy(side, number):
        source = line_ours if number == 2 else raw_ours.at[number]
        landing = (raw_ahead, raw_behind)[side]
        line = (line_ahead, line_behind)[side]
        return remote(
            source,
            line if number == 2 else landing.at[number],
            r_send.at[side, number],
            r_recv.at[side, number],
            (before_b, after_b)[side],
        )

    with jax.named_scope("raw"):
        pl.when(core == 0)(raw_first)
        pl.when(core == 1)(raw_second)
    with jax.named_scope("entry_wait"):
        pl.semaphore_wait(barrier, groups + 1 + 2 * core)

    half = groups // 2
    order = [half] + [sign * d for d in range(half - 1, 0, -1) for sign in (1, -1)]
    posts = []
    for number, distance in enumerate(order):
        posts.append(
            remote(
                stats.at[me],
                stats.at[me],
                stat_send.at[number],
                stat_recv.at[lax.rem(distance + groups, groups)],
                along(distance),
            )
        )
        posts[-1].start()

    def raw_start(side):
        for number in range(2):
            raw_copy(side, number).start()

    pl.when(core == 0)(lambda: raw_start(0))
    pl.when(core == 1)(lambda: raw_start(1))
    with jax.named_scope("stats_wait"):
        for distance in range(1, groups):
            origin = lax.rem(me - distance + groups, groups)
            ref = stats.at[origin]
            pltpu.make_async_copy(ref, ref, stat_recv.at[distance]).wait()
    total = stats[0]
    for group in range(1, groups):
        total = total + stats[group]
    count = jnp.maximum(total[0:lanes], 1.0)
    mean = total[lanes : 2 * lanes] / count
    var = total[2 * lanes : 3 * lanes] / count - mean * mean
    rate = lax.rsqrt(var + 1e-05)
    mean_line = jnp.concatenate([mean[i : i + 1] for i in range(lanes)], axis=1)
    rate_line = jnp.concatenate([rate[i : i + 1] for i in range(lanes)], axis=1)

    swap = remote(
        blocks.at[0], blocks.at[0], core_send.at[0], core_recv.at[0], other
    )

    def ahead_copy(chunk):
        return remote(
            blocks.at[0, :, pl.ds(chunk * 128, 128)],
            ahead.at[chunk],
            x_send.at[0, chunk],
            x_recv.at[0, chunk],
            before_b,
        )

    def behind_copy(chunk):
        return remote(
            ordered.at[:, pl.ds(chunk * 128, 128)],
            behind.at[chunk],
            x_send.at[1, chunk],
            x_recv.at[1, chunk],
            after_b,
        )

    def standardize(strip):
        cols = slice(strip * 128, strip * 128 + 128)
        mean_row = mean_line[:, cols]
        rate_row = rate_line[:, cols]

        def some_rows(step, carry):
            span = pl.ds(pl.multiple_of(step * 128, 128), 128)
            v = dose_v[span, cols].astype(F32)
            m = seen_v[span, cols].astype(F32)
            blocks[core, span, cols] = (m * (v - mean_row) * rate_row).astype(BF16)
            return carry

        lax.fori_loop(0, rows // 128, some_rows, 0)

    def first_core_sends():
        line_ours[0:1] = mean_line[:, 0:128]
        line_ours[1:2] = rate_line[:, 0:128]
        raw_copy(0, 2).start()
        for chunk in range(1, 4):
            standardize(chunk)
            ahead_copy(chunk).start()
        standardize(0)
        swap.start()

    def second_core_sends():
        parts = []
        for line in (mean_line, rate_line):
            for _ in range(3):
                top = line.astype(BF16)
                line = line - top.astype(F32)
                parts.append(top)
        parts = jnp.concatenate(parts + [jnp.zeros((10, width), BF16)], axis=0)
        picked = jnp.dot(parts, picks[:, 0:128], preferred_element_type=F32)
        line_ours[0:1] = picked[0:1] + picked[1:2] + picked[2:3]
        line_ours[1:2] = picked[3:4] + picked[4:5] + picked[5:6]
        raw_copy(1, 2).start()
        for strip in range(4):
            standardize(strip)
        for chunks in ((1,), (2, 3)):
            cols = slice(chunks[0] * 128, chunks[-1] * 128 + 128)
            ordered[:, cols] = jnp.dot(
                blocks[1], picks[:, cols], preferred_element_type=F32
            ).astype(BF16)
            for chunk in chunks:
                behind_copy(chunk).start()

    with jax.named_scope("standardize"):
        pl.when(core == 0)(first_core_sends)
        pl.when(core == 1)(second_core_sends)

    early = [
        Chain(
            groups,
            STRIDES[number],
            part_e.at[number],
            stage_e.at[number],
            slots_e.at[number],
            e_send.at[number],
            e_recv.at[number],
            along,
        )
        for number in range(2)
    ]
    late = [
        Chain(
            groups,
            STRIDES[2 + chunk],
            part_l.at[chunk],
            stage_l.at[chunk],
            slots_l.at[chunk],
            l_send.at[chunk],
            l_recv.at[chunk],
            along,
        )
        for chunk in range(4)
    ]

    def early_gram(number):
        if number == 1:
            with jax.named_scope("swap_wait"):
                swap.wait_recv()
        left = core if number == 0 else 0
        for strip in range(4):
            cols = slice(strip * 128, strip * 128 + 128)
            product = gram(blocks[left, :, cols], blocks[core])
            part_e[number, strip * 4 : strip * 4 + 4] = product.reshape(4, 32, 512)

    def arrived(ref, sem):
        pltpu.make_async_copy(ref, ref, sem).wait()

    def raw_standardize(side):
        raw = (raw_ahead, raw_behind)[side]
        line = (line_ahead, line_behind)[side]
        target = (ahead, behind)[side]
        with jax.named_scope("raw_wait"):
            for half in range(2):
                arrived(raw.at[half], r_recv.at[side, half])
            arrived(line, r_recv.at[side, 2])
        mean_row = line[0:1]
        rate_row = line[1:2]

        def some_rows(step, carry):
            span = pl.ds(pl.multiple_of(step * 128, 128), 128)
            v = raw[0, span].astype(F32)
            m = raw[1, span].astype(F32)
            target[0, span] = (m * (v - mean_row) * rate_row).astype(BF16)
            return carry

        lax.fori_loop(0, rows // 128, some_rows, 0)

    def late_gram(chunk):
        if chunk == 0:
            raw_standardize(0)
            raw_standardize(1)
        else:
            with jax.named_scope("ahead_wait"):
                arrived(ahead.at[chunk], x_recv.at[0, chunk])
            with jax.named_scope("behind_wait"):
                arrived(behind.at[chunk], x_recv.at[1, chunk])
        with jax.named_scope("late_gram"):
            part = part_l.at[chunk]
            for block in range(2):
                product = gram(blocks[block], ahead[chunk])
                cols = slice(block * 128, block * 128 + 128)
                part[:, :, cols] = product.reshape(16, 32, 128)
            product = gram(behind[chunk], blocks[1])
            for piece in range(4):
                cols = slice(piece * 128, piece * 128 + 128)
                part[:, piece * 8 : piece * 8 + 8, 256:384] = product[:, cols].reshape(
                    16, 8, 128
                )

    scale = 1.0 / samples
    last = chip == chips - 1

    def early_copy():
        return remote(give_e, take_e, f_send.at[0], f_recv.at[0], other)

    def late_copy(chunk):
        return remote(
            give_l.at[chunk],
            take_l.at[chunk],
            f_send.at[1 + chunk],
            f_recv.at[1 + chunk],
            other,
        )

    def back_copy(chunk):
        return remote(
            give_p.at[chunk],
            take_p.at[chunk],
            f_send.at[5 + chunk],
            f_recv.at[5 + chunk],
            before_b,
        )

    def end(number):
        if number == 0:
            out[:, 0:512] = early[0].finish() * scale
        elif number == 1:
            give_e[...] = early[1].finish() * scale
            early_copy().start()
        else:
            chunk = number - 2
            total = late[chunk].finish() * scale
            give_p[chunk] = total[:, 256:384]
            back_copy(chunk).start()
            give_l[chunk] = jnp.where(last, 0.0, total[:, 0:128])
            late_copy(chunk).start()
            cols = slice(512 + 128 * chunk, 640 + 128 * chunk)
            out[:, cols] = jnp.where(last, 0.0, total[:, 128:256])

    def first_core_end():
        arrived(take_e, f_recv.at[0])
        out[:, 512:1024] = take_e[...]
        for chunk in range(4):
            arrived(take_l.at[chunk], f_recv.at[1 + chunk])
            out[:, 1024 + 128 * chunk : 1152 + 128 * chunk] = take_l[chunk]

    def second_core_end():
        for chunk in range(4):
            arrived(take_p.at[chunk], f_recv.at[5 + chunk])
            value = jnp.where(last, 0.0, take_p[chunk])
            for piece in range(4):
                out[
                    8 * chunk : 8 * chunk + 8,
                    1024 + 128 * piece : 1152 + 128 * piece,
                ] = value[piece * 8 : piece * 8 + 8]

    def run(side):
        units = early + late
        names = ("own", "cross", "late0", "late1", "late2", "late3")
        for number, index in ORDER[side]:
            steps = units[number].levels()
            if index == 0:
                with jax.named_scope(names[number] + "_gram"):
                    if number < 2:
                        early_gram(number)
                    else:
                        late_gram(number - 2)
            with jax.named_scope(names[number] + "_" + str(index)):
                if index < len(steps):
                    for way, offset in steps[index]:
                        units[number].visit(way, offset)
                else:
                    end(number)

    def first_core():
        run(0)
        with jax.named_scope("ends"):
            first_core_end()
        swap.wait_send()
        early[0].drain()
        for chunk in range(1, 4):
            ahead_copy(chunk).wait_send()
        for number in range(3):
            raw_copy(0, number).wait_send()

    def second_core():
        run(1)
        with jax.named_scope("ends"):
            second_core_end()
        for unit in early + late:
            unit.drain()
        early_copy().wait_send()
        for chunk in range(1, 4):
            behind_copy(chunk).wait_send()
        for number in range(3):
            raw_copy(1, number).wait_send()
        for chunk in range(4):
            late_copy(chunk).wait_send()
            back_copy(chunk).wait_send()

    pl.when(core == 0)(first_core)
    pl.when(core == 1)(second_core)

    for post in posts:
        post.wait_send()


def solution(mesh):
    groups, snps = mesh.shape["samp"], mesh.shape["snp"]

    def local(dosages, observed):
        rows, width = dosages.shape
        vmem = pltpu.VMEM
        dma = pltpu.SemaphoreType.DMA
        return pl.pallas_call(
            functools.partial(band_kernel, groups, snps // 2),
            out_shape=jax.ShapeDtypeStruct((width // groups, 3 * width), F32),
            in_specs=[pl.BlockSpec(memory_space=pl.ANY)] * 2,
            out_specs=pl.BlockSpec(memory_space=pltpu.VMEM),
            scratch_shapes=[
                vmem((rows, width), BF16),
                vmem((rows, width), jnp.int32),
                vmem((groups, 16, 128), F32),
                vmem((2, rows, width), BF16),
                vmem((width, width), BF16),
                vmem((rows, width), BF16),
                vmem((4, rows, 128), BF16),
                vmem((4, rows, 128), BF16),
                vmem((2, rows, 128), BF16),
                vmem((2, rows, 128), BF16),
                vmem((2, rows, 128), BF16),
                vmem((8, 128), F32),
                vmem((8, 128), F32),
                vmem((8, 128), F32),
                vmem((2, groups, 32, 512), F32),
                vmem((4, groups, 32, 384), F32),
                vmem((2, 2, 8, 32, 512), jnp.int16),
                vmem((4, 2, 8, 32, 384), jnp.int16),
                vmem((2, 2, 8, 32, 512), jnp.int16),
                vmem((4, 2, 8, 32, 384), jnp.int16),
                vmem((32, 512), F32),
                vmem((4, 32, 128), F32),
                vmem((4, 32, 128), F32),
                vmem((32, 512), F32),
                vmem((4, 32, 128), F32),
                vmem((4, 32, 128), F32),
                dma((2, 6)),
                dma((groups,)),
                dma((groups,)),
                dma((1,)),
                dma((1,)),
                dma((2, 4)),
                dma((2, 4)),
                dma((2, 3)),
                dma((2, 3)),
                dma((2, 2, 8)),
                dma((2, 2, 8)),
                dma((4, 2, 8)),
                dma((4, 2, 8)),
                dma((9,)),
                dma((9,)),
            ],
            compiler_params=pltpu.CompilerParams(
                collective_id=0,
                has_side_effects=True,
                vmem_limit_bytes=56 * 2**20,
            ),
            cost_estimate=pl.CostEstimate(
                flops=2 * 3 * rows * width * width,
                bytes_accessed=6 * rows * width,
                transcendentals=0,
            ),
            name="band",
        )(dosages, observed)

    return jax.shard_map(
        local,
        mesh=mesh,
        in_specs=(P("samp", "snp"), P("samp", "snp")),
        out_specs=P(("snp", "samp"), None),
        check_vma=False,
    )
```

time: 80.4 us -> 66.6 us (0.83)
  Pallas kernels: 78.6 us -> 64.8 us
    pallas_call x1, Pallas kernels: 78.6 us -> 64.8 us  [local(): pl.pallas_call(functools.partial(band_kernel, groups, snps // 2), out_sha...]
where the time goes in v2:
time: 66.6 us; the launch traced here: 66.4 us
  Pallas kernels  64.8 us (97%)
  local copies, waits for them, and re-layouts  1.62 us (2%)
    pallas_call x1, Pallas kernels, local(): pl.pallas_call(functools.partial(band_kernel, groups, snps // 2), out_sha...  64.8 us
    unnamed x1, local copies, waits for them, and re-layouts  1.62 us

profile of v2, /device:TPU:1, one launch (start us, length us, event | category | flops | bytes accessed | tf_op | source)
XLA Modules:
  0.0 66.4 jit_solution(1070943025010872178)
XLA Ops:
  0.0 64.8 %band.1 = f32[32,1536]{1,0:T(8,128)} custom-call(bf16[1536,512]{1,0:T(8,128)(2,1)} %dosages.1, s32[1536,512]{1,0:T(8,128)} %observed.1), custom_call_target="tpu_custom_call" | custom-call | flops 2415919104 | bytes 4718592 | tf_op jit(solution)/shard_map/band/pallas_call | solution.py:584
  64.8 1.6 %copy.4 = f32[32,1536]{1,0:T(8,128)} copy(f32[32,1536]{1,0:T(8,128)} %band.1) | data formatting | bytes 393216

commit v3 on v2

v3 whole, which is shorter than its diff:
```python
import functools
import math

import jax
import jax.numpy as jnp
from jax import lax
from jax.experimental import pallas as pl
from jax.experimental.pallas import tpu as pltpu
from jax.sharding import PartitionSpec as P

MESH = pl.DeviceIdType.MESH
F32 = jnp.float32
BF16 = jnp.bfloat16

STEPS = 1650.0
FINE = 4096.0


OWN_STRIDE = 1
CROSS = 1
CROSS_STRIDE = 1
LATE = ((0, 0, 32, 1), (1, 0, 32, 1), (2, 0, 32, 1), (3, 0, 32, 2))
ORDER = (
    ((0, 0), (0, 1), (0, 2), (0, 3), (0, 4), (0, 5), (0, 6), (0, 7), (0, 8),),
    ((0, 0), (0, 1), (1, 0), (3, 0), (2, 0), (1, 1), (3, 1), (0, 2), (4, 0), (2, 1), (1, 2), (3, 2), (0, 3), (4, 1), (2, 2), (1, 3), (5, 0), (4, 2), (3, 3), (2, 3), (1, 4), (0, 4), (4, 3), (3, 4), (2, 4), (1, 5), (0, 5), (5, 1), (4, 4), (3, 5), (2, 5), (1, 6), (0, 6), (4, 5), (5, 2), (3, 6), (2, 6), (1, 7), (0, 7), (4, 6), (3, 7), (2, 7), (5, 3), (1, 8), (0, 8), (4, 7), (3, 8), (2, 8), (5, 4), (4, 8),),
)


def encode(x):
    q = jnp.minimum(STEPS * jnp.log(1.0 + FINE * jnp.abs(x)) + 0.5, 32767.0).astype(
        jnp.int32
    )
    return jnp.where(x < 0.0, -q, q).astype(jnp.int16)


def decode(q):
    f = q.astype(jnp.int32).astype(F32)
    a = (jnp.exp(jnp.abs(f) * (1.0 / STEPS)) - 1.0) * (1.0 / FINE)
    return jnp.where(f < 0.0, -a, a)


def gram(left, right):
    return lax.dot_general(
        left, right, (((0,), (0,)), ((), ())), preferred_element_type=F32
    )


class Chain:
    def __init__(self, groups, stride, part, stage, slots, send, recv, device, last=None):
        self.groups = groups
        self.reach = (groups // 2, groups - 1 - groups // 2)
        self.stride = tuple(min(stride, reach) for reach in self.reach)
        self.part, self.stage, self.slots = part, stage, slots
        self.send, self.recv, self.device, self.last = send, recv, device, last

    def slot(self, way, number):
        return way * self.reach[0] + number - 1

    def hops(self, way, offset, source):
        stride, reach = self.stride[way], self.reach[way]
        sign = 1 if way == 0 else -1
        slot = offset - stride if offset > stride else reach - stride + offset
        slot = self.slot(way, slot)
        if offset > stride or self.last is None:
            return [
                pltpu.make_async_remote_copy(
                    src_ref=source,
                    dst_ref=self.slots.at[slot],
                    send_sem=self.send,
                    recv_sem=self.recv.at[slot],
                    device_id=self.device(sign * min(stride, offset)),
                    device_id_type=MESH,
                )
            ]
        return self.last(slot, sign * offset, source)

    def arrival(self, way, number):
        slot = self.slot(way, number)
        ref = self.slots.at[slot]
        return pltpu.make_async_copy(ref, ref, self.recv.at[slot])

    def own(self, way, offset):
        me = lax.axis_index("samp")
        sign = 1 if way == 0 else -1
        return lax.rem(me + sign * offset + self.groups, self.groups)

    def source(self, way, offset):
        reach, stride = self.reach[way], self.stride[way]
        if offset + stride > reach:
            return self.stage.at[way, reach - offset]
        return self.slots.at[self.slot(way, offset)]

    def last_slots(self):
        return [
            self.slot(way, self.reach[way] - self.stride[way] + near)
            for near in range(1, max(self.stride) + 1)
            for way in (0, 1)
            if near <= self.stride[way]
        ]

    def visit(self, way, offset):
        reach, stride = self.reach[way], self.stride[way]
        ref = self.source(way, offset)
        total = self.part[self.own(way, offset)]
        if offset + stride <= reach:
            self.arrival(way, offset).wait()
            total = total + decode(ref[...])
        ref[...] = encode(total)
        for copy in self.hops(way, offset, ref):
            copy.start()

    def levels(self):
        steps = []
        for way in (0, 1):
            for place, offset in enumerate(range(self.reach[way], 0, -1)):
                number = place // self.stride[way]
                if number == len(steps):
                    steps.append([])
                steps[number].append((place, way, offset))
        return [[visit[1:] for visit in sorted(step)] for step in steps]

    def finish(self):
        total = self.part[lax.axis_index("samp")]
        for slot in self.last_slots():
            ref = self.slots.at[slot]
            pltpu.make_async_copy(ref, ref, self.recv.at[slot]).wait()
            total = total + decode(ref[...])
        return total

    def drain(self, last_send=None):
        whole, end = sum(self.reach), sum(self.stride)
        if last_send is not None:
            ref = self.slots.at[pl.ds(0, end)]
            pltpu.make_async_copy(ref, ref, last_send).wait()
            whole -= end
        if whole:
            ref = self.slots.at[pl.ds(0, whole)]
            pltpu.make_async_copy(ref, ref, self.send).wait()


LATE_ENDS = [
    Chain(16, unit[3], None, None, None, None, None, None).last_slots() for unit in LATE
]
LATE_FROM = [sum(len(e) for e in LATE_ENDS[:n]) for n in range(len(LATE) + 1)]


def band_kernel(
    groups,
    chips,
    dosages,
    observed,
    out,
    dose_v,
    seen_v,
    stats,
    blocks,
    picks,
    ordered,
    ahead,
    behind,
    raw_ours,
    raw_ahead,
    raw_behind,
    line_ours,
    line_ahead,
    line_behind,
    part_e,
    part_l,
    stage_e,
    stage_l,
    slots_e,
    slots_l,
    ours_l,
    home_l,
    give_e,
    take_e,
    load_sem,
    stat_send,
    stat_recv,
    core_send,
    core_recv,
    x_send,
    x_recv,
    r_send,
    r_recv,
    e_send,
    e_recv,
    l_send,
    l_recv,
    t_send,
    t_recv,
    h_send,
    h_recv,
    f_send,
    f_recv,
):
    snp, me = lax.axis_index("snp"), lax.axis_index("samp")
    core = lax.rem(snp, 2)
    chip = lax.div(snp, 2)
    rows, width = dose_v.shape
    samples = rows * groups
    count_snp = 2 * chips

    def along(distance):
        return (snp, lax.rem(me + distance + groups, groups))

    other = (snp + 1 - 2 * core, me)
    before_b = (lax.rem(2 * chip + count_snp - 1, count_snp), me)
    after_b = (lax.rem(2 * chip + 3, count_snp), me)
    after_a = (lax.rem(2 * chip + 2, count_snp), me)

    def remote(src, dst, send, recv, device):
        return pltpu.make_async_remote_copy(
            src_ref=src,
            dst_ref=dst,
            send_sem=send,
            recv_sem=recv,
            device_id=device,
            device_id_type=MESH,
        )

    half = groups // 2
    order = [half] + [sign * d for d in range(half - 1, 0, -1) for sign in (1, -1)]
    barrier = pltpu.get_barrier_semaphore()

    def greet(peers):
        for peer in peers:
            pl.semaphore_signal(barrier, inc=1, device_id=peer, device_id_type=MESH)

    def beside(device, distance):
        return (device[0], lax.rem(me + distance + groups, groups))

    greet([along(d) for d in order] + [other, before_b])
    pl.when(core == 1)(lambda: greet([after_a, after_b]))

    pieces = load_sem.shape[1]
    high = rows // pieces

    def load(piece):
        span = pl.ds(piece * high, high)
        return (
            pltpu.make_async_copy(
                dosages.at[span], dose_v.at[span], load_sem.at[0, piece]
            ),
            pltpu.make_async_copy(
                observed.at[span], seen_v.at[span], load_sem.at[1, piece]
            ),
        )


    for piece in range(pieces):
        for copy in load(piece):
            copy.start()

    def make_picks():
        line = lax.broadcasted_iota(jnp.int32, (width, width), 0)
        col = lax.broadcasted_iota(jnp.int32, (width, width), 1)
        from_row = 32 * ((col >> 3) & 15) + 8 * (col >> 7) + (col & 7)
        picks[...] = jnp.where(line == from_row, 1.0, 0.0).astype(BF16)

    def add_rows(step, carry):
        span = pl.ds(pl.multiple_of(step * 32, 32), 32)
        v = dose_v[span].astype(F32)
        m = seen_v[span].astype(F32)
        mv = m * v
        sums = []
        for acc, term in zip(carry, (m, mv, mv * v)):
            sums.append(acc + jnp.sum(term.reshape(4, 8, width), axis=0))
        return tuple(sums)

    carry = tuple(jnp.zeros((8, width), F32) for _ in range(3))
    for piece in range(pieces):
        for copy in load(piece):
            copy.wait()
        carry = lax.fori_loop(
            piece * high // 32, (piece + 1) * high // 32, add_rows, carry
        )
    lanes = width // 128
    for kind, acc in enumerate(carry):
        line = jnp.sum(acc, axis=0, keepdims=True)
        for lane in range(lanes):
            row = kind * lanes + lane
            stats[me, row : row + 1, :] = line[:, lane * 128 : lane * 128 + 128]

    def raw_first():
        raw_ours[0] = dose_v[:, 0:128]
        raw_ours[1] = seen_v[:, 0:128].astype(F32).astype(BF16)

    def raw_second():
        make_picks()
        pick = picks[:, 0:128]
        raw_ours[0] = jnp.dot(
            dose_v[...], pick, preferred_element_type=F32
        ).astype(BF16)
        raw_ours[1] = jnp.dot(
            seen_v[...].astype(F32).astype(BF16), pick, preferred_element_type=F32
        ).astype(BF16)

    def raw_copy(side, number):
        return remote(
            (raw_ours, line_ours)[number],
            ((raw_ahead, raw_behind), (line_ahead, line_behind))[number][side],
            r_send.at[number],
            r_recv.at[side, number],
            (before_b, after_b)[side],
        )

    with jax.named_scope("raw"):
        pl.when(core == 0)(raw_first)
        pl.when(core == 1)(raw_second)
    with jax.named_scope("entry_wait"):
        pl.semaphore_wait(barrier, groups + 1 + 2 * core)

    posts = []
    for distance in order:
        posts.append(
            remote(
                stats.at[me],
                stats.at[me],
                stat_send,
                stat_recv.at[lax.rem(distance + groups, groups)],
                along(distance),
            )
        )
        posts[-1].start()

    pl.when(core == 0)(lambda: raw_copy(0, 0).start())
    pl.when(core == 1)(lambda: raw_copy(1, 0).start())
    with jax.named_scope("stats_wait"):
        for distance in range(1, groups):
            origin = lax.rem(me - distance + groups, groups)
            ref = stats.at[origin]
            pltpu.make_async_copy(ref, ref, stat_recv.at[distance]).wait()
    total = stats[0]
    for group in range(1, groups):
        total = total + stats[group]
    count = jnp.maximum(total[0:lanes], 1.0)
    mean = total[lanes : 2 * lanes] / count
    var = total[2 * lanes : 3 * lanes] / count - mean * mean
    rate = lax.rsqrt(var + 1e-05)
    mean_line = jnp.concatenate([mean[i : i + 1] for i in range(lanes)], axis=1)
    rate_line = jnp.concatenate([rate[i : i + 1] for i in range(lanes)], axis=1)

    def arrived(ref, sem):
        pltpu.make_async_copy(ref, ref, sem).wait()

    def swap(block):
        return remote(
            blocks.at[block],
            blocks.at[block],
            core_send,
            core_recv,
            other,
        )

    def ahead_copy(chunk):
        return remote(
            blocks.at[0, :, pl.ds(chunk * 128, 128)],
            ahead.at[chunk],
            x_send,
            x_recv.at[0, chunk - 1],
            before_b,
        )

    def behind_copy(chunk):
        return remote(
            ordered.at[:, pl.ds(chunk * 128, 128)],
            behind.at[chunk],
            x_send,
            x_recv.at[1, chunk - 1],
            after_b,
        )

    def standardize(strip):
        cols = slice(strip * 128, strip * 128 + 128)
        mean_row = mean_line[:, cols]
        rate_row = rate_line[:, cols]

        def some_rows(step, carry):
            span = pl.ds(pl.multiple_of(step * 128, 128), 128)
            v = dose_v[span, cols].astype(F32)
            m = seen_v[span, cols].astype(F32)
            blocks[core, span, cols] = (m * (v - mean_row) * rate_row).astype(BF16)
            return carry

        lax.fori_loop(0, rows // 128, some_rows, 0)

    def first_core_sends():
        line_ours[0:1] = mean_line[:, 0:128]
        line_ours[1:2] = rate_line[:, 0:128]
        raw_copy(0, 1).start()
        for chunk in range(1, 4):
            standardize(chunk)
            ahead_copy(chunk).start()
        standardize(0)
        swap(0).start()

    def second_core_sends():
        parts = []
        for line in (mean_line, rate_line):
            for _ in range(3):
                top = line.astype(BF16)
                line = line - top.astype(F32)
                parts.append(top)
        parts = jnp.concatenate(parts + [jnp.zeros((10, width), BF16)], axis=0)
        picked = jnp.dot(parts, picks[:, 0:128], preferred_element_type=F32)
        line_ours[0:1] = picked[0:1] + picked[1:2] + picked[2:3]
        line_ours[1:2] = picked[3:4] + picked[4:5] + picked[5:6]
        raw_copy(1, 1).start()
        for strip in range(4):
            standardize(strip)
        for chunks in ((1,), (2, 3)):
            cols = slice(chunks[0] * 128, chunks[-1] * 128 + 128)
            ordered[:, cols] = jnp.dot(
                blocks[1], picks[:, cols], preferred_element_type=F32
            ).astype(BF16)
            for chunk in chunks:
                behind_copy(chunk).start()
            if CROSS == 0 and chunks[0] == 1:
                swap(1).start()

    with jax.named_scope("standardize"):
        pl.when(core == 0)(first_core_sends)
        pl.when(core == 1)(second_core_sends)

    early = [
        Chain(
            groups,
            (OWN_STRIDE, CROSS_STRIDE)[number],
            part_e.at[number],
            stage_e.at[number],
            slots_e.at[number],
            e_send.at[number],
            e_recv.at[number],
            along,
        )
        for number in range(2)
    ]
    def end_sem(unit, third, slot):
        if third < 2:
            return l_recv.at[unit, slot]
        return t_recv.at[LATE_ENDS[unit].index(slot) + LATE_FROM[unit]]

    def thirds(unit):
        chunk, first, high, _ = LATE[unit]
        line = pl.ds(first, high)

        def last(slot, distance, source):
            homes = (beside(other, distance), along(distance), beside(before_b, distance))
            return [
                remote(
                    source.at[:, pl.ds(128 * third, 128)],
                    slots_l.at[chunk, slot, line, pl.ds(128 * third, 128)],
                    t_send.at[unit],
                    end_sem(unit, third, slot),
                    homes[third],
                )
                for third in range(3)
            ]

        return last

    late = [
        Chain(
            groups,
            stride,
            part_l.at[chunk, :, pl.ds(first, high)],
            stage_l.at[chunk, :, :, pl.ds(first, high)],
            slots_l.at[chunk, :, pl.ds(first, high)],
            l_send.at[unit],
            l_recv.at[unit],
            along,
            thirds(unit),
        )
        for unit, (chunk, first, high, stride) in enumerate(LATE)
    ]

    def own_term(chunk, third):
        cols = pl.ds(128 * third, 128)
        return remote(
            ours_l.at[chunk, :, cols],
            home_l.at[chunk, :, cols],
            h_send,
            h_recv.at[chunk],
            other if third == 0 else before_b,
        )

    def landed(unit, third):
        chunk, first, high, _ = LATE[unit]
        total = jnp.zeros((high, 128), F32)
        for slot in late[unit].last_slots():
            ref = slots_l.at[
                chunk, slot, pl.ds(first, high), pl.ds(128 * third, 128)
            ]
            arrived(ref, end_sem(unit, third, slot))
            total = total + decode(ref[...])
        return total

    def early_gram(number):
        left, right = (core, core) if number == 0 else (0, 1)
        for strip in range(4):
            cols = slice(strip * 128, strip * 128 + 128)
            product = gram(blocks[left, :, cols], blocks[right])
            part_e[number, strip * 4 : strip * 4 + 4] = product.reshape(4, 32, 512)

    def raw_standardize(side):
        raw = (raw_ahead, raw_behind)[side]
        line = (line_ahead, line_behind)[side]
        target = (ahead, behind)[side]
        with jax.named_scope("raw_wait"):
            arrived(raw, r_recv.at[side, 0])
            arrived(line, r_recv.at[side, 1])
        mean_row = line[0:1]
        rate_row = line[1:2]

        def some_rows(step, carry):
            span = pl.ds(pl.multiple_of(step * 128, 128), 128)
            v = raw[0, span].astype(F32)
            m = raw[1, span].astype(F32)
            target[0, span] = (m * (v - mean_row) * rate_row).astype(BF16)
            return carry

        lax.fori_loop(0, rows // 128, some_rows, 0)

    def late_gram(chunk):
        if chunk == 0:
            raw_standardize(0)
            raw_standardize(1)
        else:
            with jax.named_scope("ahead_wait"):
                arrived(ahead.at[chunk], x_recv.at[0, chunk - 1])
            with jax.named_scope("behind_wait"):
                arrived(behind.at[chunk], x_recv.at[1, chunk - 1])
        with jax.named_scope("late_gram"):
            part = part_l.at[chunk]
            for block in range(2):
                product = gram(blocks[block], ahead[chunk])
                cols = slice(block * 128, block * 128 + 128)
                part[:, :, cols] = product.reshape(16, 32, 128)
            product = gram(behind[chunk], blocks[1])
            for piece in range(4):
                cols = slice(piece * 128, piece * 128 + 128)
                part[:, piece * 8 : piece * 8 + 8, 256:384] = product[:, cols].reshape(
                    16, 8, 128
                )
            ours_l[chunk] = encode(part[me])
            own_term(chunk, 0).start()
            own_term(chunk, 2).start()

    scale = 1.0 / samples
    last = chip == chips - 1

    def early_copy():
        return remote(give_e, take_e, f_send.at[0], f_recv.at[0], other)

    def end(number):
        if number == 0:
            out[:, 0:512] = early[0].finish() * scale
        elif number == 1:
            total = early[1].finish() * scale
            if CROSS == 0:
                out[:, 512:1024] = total
            else:
                give_e[...] = total
                early_copy().start()
        else:
            unit = number - 2
            chunk, first, high, _ = LATE[unit]
            line = slice(first, first + high)
            total = landed(unit, 1) + part_l[chunk, me, line, 128:256]
            cols = slice(512 + 128 * chunk, 640 + 128 * chunk)
            out[line, cols] = jnp.where(last, 0.0, total * scale)

    def end_first(unit):
        chunk, first, high, _ = LATE[unit]
        line = slice(first, first + high)
        if unit == 0 or LATE[unit - 1][0] != chunk:
            arrived(home_l.at[chunk, :, pl.ds(0, 128)], h_recv.at[chunk])
        total = landed(unit, 0) + decode(home_l[chunk, line, 0:128])
        cols = slice(1024 + 128 * chunk, 1152 + 128 * chunk)
        out[line, cols] = jnp.where(last, 0.0, total * scale)

    def end_second(unit):
        chunk, first, high, _ = LATE[unit]
        line = slice(first, first + high)
        if unit == 0 or LATE[unit - 1][0] != chunk:
            arrived(home_l.at[chunk, :, pl.ds(256, 128)], h_recv.at[chunk])
        total = landed(unit, 2) + decode(home_l[chunk, line, 256:384])
        value = jnp.where(last, 0.0, total * scale)
        for piece in range(high // 8):
            cols = 1024 + 128 * (first // 8 + piece)
            out[8 * chunk : 8 * chunk + 8, cols : cols + 128] = value[
                piece * 8 : piece * 8 + 8
            ]

    def run(side):
        units = early + late
        swapped = False
        for number, index in ORDER[side]:
            name = ("own", "cross")[number] if number < 2 else f"late{number - 2}"
            steps = units[number].levels()
            if number > 0 and not swapped:
                swapped = True
                if side == 1 or CROSS == 0:
                    with jax.named_scope("swap_wait"):
                        swap(1 - side).wait_recv()
            if index == 0:
                with jax.named_scope(name + "_gram"):
                    if number < 2:
                        early_gram(number)
                    elif number == 2 or LATE[number - 3][0] != LATE[number - 2][0]:
                        late_gram(LATE[number - 2][0])
            with jax.named_scope(f"{name}_{index}"):
                if index < len(steps):
                    for way, offset in steps[index]:
                        units[number].visit(way, offset)
                else:
                    end(number)

    def first_core():
        run(0)
        with jax.named_scope("ends"):
            for unit in range(len(LATE)):
                end_first(unit)
            if CROSS == 1:
                arrived(take_e, f_recv.at[0])
                out[:, 512:1024] = take_e[...]
        swap(0).wait_send()
        for chain in early[: 2 - CROSS]:
            chain.drain()
        arrived(ahead.at[pl.ds(0, 3)], x_send)
        for number in range(2):
            raw_copy(0, number).wait_send()

    def second_core():
        run(1)
        with jax.named_scope("ends"):
            for unit in range(len(LATE)):
                end_second(unit)
        for chain in early[: 1 + CROSS]:
            chain.drain()
        for unit, chain in enumerate(late):
            chain.drain(t_send.at[unit])
        if CROSS == 1:
            early_copy().wait_send()
        else:
            swap(1).wait_send()
        arrived(ahead.at[pl.ds(0, 3)], x_send)
        for number in range(2):
            raw_copy(1, number).wait_send()
        arrived(ours_l.at[:, :, pl.ds(0, 256)], h_send)

    pl.when(core == 0)(first_core)
    pl.when(core == 1)(second_core)

    sent = stats.at[pl.ds(0, groups - 1)]
    pltpu.make_async_copy(sent, sent, stat_send).wait()


def solution(mesh):
    groups, snps = mesh.shape["samp"], mesh.shape["snp"]

    def local(dosages, observed):
        rows, width = dosages.shape
        vmem = pltpu.VMEM
        dma = pltpu.SemaphoreType.DMA
        return pl.pallas_call(
            functools.partial(band_kernel, groups, snps // 2),
            out_shape=jax.ShapeDtypeStruct((width // groups, 3 * width), F32),
            in_specs=[pl.BlockSpec(memory_space=pl.ANY)] * 2,
            out_specs=pl.BlockSpec(memory_space=pltpu.VMEM),
            scratch_shapes=[
                vmem((rows, width), BF16),
                vmem((rows, width), jnp.int32),
                vmem((groups, 12, 128), F32),
                vmem((2, rows, width), BF16),
                vmem((width, width), BF16),
                vmem((rows, width), BF16),
                vmem((4, rows, 128), BF16),
                vmem((4, rows, 128), BF16),
                vmem((2, rows, 128), BF16),
                vmem((2, rows, 128), BF16),
                vmem((2, rows, 128), BF16),
                vmem((8, 128), F32),
                vmem((8, 128), F32),
                vmem((8, 128), F32),
                vmem((2, groups, 32, 512), F32),
                vmem((4, groups, 32, 384), F32),
                vmem((2, 2, 8, 32, 512), jnp.int16),
                vmem((4, 2, 8, 32, 384), jnp.int16),
                vmem((2, 15, 32, 512), jnp.int16),
                vmem((4, 15, 32, 384), jnp.int16),
                vmem((4, 32, 384), jnp.int16),
                vmem((4, 32, 384), jnp.int16),
                vmem((32, 512), F32),
                vmem((32, 512), F32),
                dma((2, 4)),
                dma,
                dma((groups,)),
                dma,
                dma,
                dma,
                dma((2, 3)),
                dma((2,)),
                dma((2, 2)),
                dma((2,)),
                dma((2, 15)),
                dma((len(LATE),)),
                dma((len(LATE), 15)),
                dma((len(LATE),)),
                dma((LATE_FROM[-1],)),
                dma,
                dma((4,)),
                dma((1,)),
                dma((1,)),
            ],
            compiler_params=pltpu.CompilerParams(
                collective_id=0,
                has_side_effects=True,
                vmem_limit_bytes=56 * 2**20,
            ),
            cost_estimate=pl.CostEstimate(
                flops=2 * 3 * rows * width * width,
                bytes_accessed=6 * rows * width,
                transcendentals=0,
            ),
            name="band",
        )(dosages, observed)

    return jax.shard_map(
        local,
        mesh=mesh,
        in_specs=(P("samp", "snp"), P("samp", "snp")),
        out_specs=P(("snp", "samp"), None),
        check_vma=False,
    )
```

time: 66.6 us -> 64.7 us (0.971)
  Pallas kernels: 64.8 us -> 62.9 us
    pallas_call x1, Pallas kernels: 64.8 us -> 62.9 us  [local(): pl.pallas_call(functools.partial(band_kernel, groups, snps // 2), out_sha...]
where the time goes in v3:
time: 64.7 us; the launch traced here: 64.6 us
  Pallas kernels  62.9 us (97%)
  local copies, waits for them, and re-layouts  1.62 us (3%)
    pallas_call x1, Pallas kernels, local(): pl.pallas_call(functools.partial(band_kernel, groups, snps // 2), out_sha...  62.9 us
    unnamed x1, local copies, waits for them, and re-layouts  1.62 us

profile of v3, /device:TPU:1, one launch (start us, length us, event | category | flops | bytes accessed | tf_op | source)
XLA Modules:
  0.0 64.6 jit_solution(15327727140266969472)
XLA Ops:
  0.0 62.9 %band.1 = f32[32,1536]{1,0:T(8,128)} custom-call(bf16[1536,512]{1,0:T(8,128)(2,1)} %dosages.1, s32[1536,512]{1,0:T(8,128)} %observed.1), custom_call_target="tpu_custom_call" | custom-call | flops 2415919104 | bytes 4718592 | tf_op jit(solution)/shard_map/band/pallas_call | solution.py:667
  62.9 1.6 %copy.4 = f32[32,1536]{1,0:T(8,128)} copy(f32[32,1536]{1,0:T(8,128)} %band.1) | data formatting | bytes 393216

commit v4 on v3

--- a/solution.py
+++ b/solution.py
@@ -16,13 +16,13 @@
 FINE = 4096.0
 
 
-OWN_STRIDE = 1
+OWN_STRIDE = 2
 CROSS = 1
 CROSS_STRIDE = 1
-LATE = ((0, 0, 32, 1), (1, 0, 32, 1), (2, 0, 32, 1), (3, 0, 32, 2))
+LATE = ((0, 0, 32, 1), (1, 0, 32, 1), (2, 0, 32, 2), (3, 0, 32, 2))
 ORDER = (
-    ((0, 0), (0, 1), (0, 2), (0, 3), (0, 4), (0, 5), (0, 6), (0, 7), (0, 8),),
-    ((0, 0), (0, 1), (1, 0), (3, 0), (2, 0), (1, 1), (3, 1), (0, 2), (4, 0), (2, 1), (1, 2), (3, 2), (0, 3), (4, 1), (2, 2), (1, 3), (5, 0), (4, 2), (3, 3), (2, 3), (1, 4), (0, 4), (4, 3), (3, 4), (2, 4), (1, 5), (0, 5), (5, 1), (4, 4), (3, 5), (2, 5), (1, 6), (0, 6), (4, 5), (5, 2), (3, 6), (2, 6), (1, 7), (0, 7), (4, 6), (3, 7), (2, 7), (5, 3), (1, 8), (0, 8), (4, 7), (3, 8), (2, 8), (5, 4), (4, 8),),
+    ((0, 0), (0, 1), (0, 2), (0, 3), (0, 4),),
+    ((0, 0), (1, 0), (2, 0), (3, 0), (1, 1), (0, 1), (2, 1), (4, 0), (3, 1), (1, 2), (2, 2), (0, 2), (5, 0), (3, 2), (2, 3), (1, 3), (4, 1), (0, 3), (3, 3), (2, 4), (1, 4), (5, 1), (3, 4), (2, 5), (4, 2), (0, 4), (1, 5), (5, 2), (3, 5), (2, 6), (1, 6), (4, 3), (3, 6), (2, 7), (5, 3), (1, 7), (4, 4), (3, 7), (2, 8), (1, 8), (5, 4), (3, 8),),
 )
 
 
@@ -159,6 +159,7 @@
     ahead,
     behind,
     raw_ours,
+    raw_rest,
     raw_ahead,
     raw_behind,
     line_ours,
@@ -209,6 +210,10 @@
     after_b = (lax.rem(2 * chip + 3, count_snp), me)
     after_a = (lax.rem(2 * chip + 2, count_snp), me)
 
+    has_before, has_after = chip > 0, chip < chips - 1
+    sends_ahead = jnp.logical_and(core == 0, has_before)
+    sends_behind = jnp.logical_and(core == 1, has_after)
+
     def remote(src, dst, send, recv, device):
         return pltpu.make_async_remote_copy(
             src_ref=src,
@@ -285,16 +290,26 @@
     def raw_first():
         raw_ours[0] = dose_v[:, 0:128]
         raw_ours[1] = seen_v[:, 0:128].astype(F32).astype(BF16)
+        pl.when(has_before)(raw_copy(0, 0).start)
 
     def raw_second():
-        make_picks()
-        pick = picks[:, 0:128]
+        ordered[...] = seen_v[...].astype(F32).astype(BF16)
+        first = picks[:, 0:128]
         raw_ours[0] = jnp.dot(
-            dose_v[...], pick, preferred_element_type=F32
+            dose_v[...], first, preferred_element_type=F32
         ).astype(BF16)
         raw_ours[1] = jnp.dot(
-            seen_v[...].astype(F32).astype(BF16), pick, preferred_element_type=F32
+            ordered[...], first, preferred_element_type=F32
         ).astype(BF16)
+        pl.when(has_after)(raw_copy(1, 0).start)
+        for pair in (slice(128, 256), slice(256, 512)):
+            cols = slice(pair.start - 128, pair.stop - 128)
+            raw_rest[0, :, cols] = jnp.dot(
+                dose_v[...], picks[:, pair], preferred_element_type=F32
+            ).astype(BF16)
+            raw_rest[1, :, cols] = jnp.dot(
+                ordered[...], picks[:, pair], preferred_element_type=F32
+            ).astype(BF16)
 
     def raw_copy(side, number):
         return remote(
@@ -305,9 +320,16 @@
             (before_b, after_b)[side],
         )
 
-    with jax.named_scope("raw"):
-        pl.when(core == 0)(raw_first)
-        pl.when(core == 1)(raw_second)
+    def no_after():
+        ahead[...] = jnp.zeros(ahead.shape, BF16)
+
+    def no_before():
+        behind[...] = jnp.zeros(behind.shape, BF16)
+
+    pl.when(jnp.logical_and(core == 1, jnp.logical_not(has_after)))(no_after)
+    pl.when(jnp.logical_and(core == 1, jnp.logical_not(has_before)))(no_before)
+
+    pl.when(core == 1)(make_picks)
     with jax.named_scope("entry_wait"):
         pl.semaphore_wait(barrier, groups + 1 + 2 * core)
 
@@ -324,8 +346,9 @@
         )
         posts[-1].start()
 
-    pl.when(core == 0)(lambda: raw_copy(0, 0).start())
-    pl.when(core == 1)(lambda: raw_copy(1, 0).start())
+    with jax.named_scope("raw"):
+        pl.when(core == 0)(raw_first)
+        pl.when(core == 1)(raw_second)
     with jax.named_scope("stats_wait"):
         for distance in range(1, groups):
             origin = lax.rem(me - distance + groups, groups)
@@ -353,6 +376,16 @@
             other,
         )
 
+    def swap_strip(strip):
+        cols = pl.ds(strip * 128, 128)
+        return remote(
+            blocks.at[0, :, cols],
+            blocks.at[0, :, cols],
+            core_send,
+            core_recv,
+            other,
+        )
+
     def ahead_copy(chunk):
         return remote(
             blocks.at[0, :, pl.ds(chunk * 128, 128)],
@@ -388,12 +421,13 @@
     def first_core_sends():
         line_ours[0:1] = mean_line[:, 0:128]
         line_ours[1:2] = rate_line[:, 0:128]
-        raw_copy(0, 1).start()
+        pl.when(sends_ahead)(lambda: raw_copy(0, 1).start())
         for chunk in range(1, 4):
             standardize(chunk)
-            ahead_copy(chunk).start()
+            pl.when(sends_ahead)(ahead_copy(chunk).start)
+            swap_strip(chunk).start()
         standardize(0)
-        swap(0).start()
+        swap_strip(0).start()
 
     def second_core_sends():
         parts = []
@@ -403,21 +437,30 @@
                 line = line - top.astype(F32)
                 parts.append(top)
         parts = jnp.concatenate(parts + [jnp.zeros((10, width), BF16)], axis=0)
-        picked = jnp.dot(parts, picks[:, 0:128], preferred_element_type=F32)
-        line_ours[0:1] = picked[0:1] + picked[1:2] + picked[2:3]
-        line_ours[1:2] = picked[3:4] + picked[4:5] + picked[5:6]
-        raw_copy(1, 1).start()
+        picked = jnp.dot(parts, picks[...], preferred_element_type=F32)
+        mean_row = picked[0:1] + picked[1:2] + picked[2:3]
+        rate_row = picked[3:4] + picked[4:5] + picked[5:6]
+        line_ours[0:1] = mean_row[:, 0:128]
+        line_ours[1:2] = rate_row[:, 0:128]
+        pl.when(sends_behind)(lambda: raw_copy(1, 1).start())
+        for chunk in range(1, 4):
+            cols = slice(128 * chunk, 128 * chunk + 128)
+            rest = slice(128 * chunk - 128, 128 * chunk)
+
+            def some_rows(step, carry):
+                span = pl.ds(pl.multiple_of(step * 128, 128), 128)
+                v = raw_rest[0, span, rest].astype(F32)
+                m = raw_rest[1, span, rest].astype(F32)
+                z = m * (v - mean_row[:, cols]) * rate_row[:, cols]
+                ordered[span, cols] = z.astype(BF16)
+                return carry
+
+            lax.fori_loop(0, rows // 128, some_rows, 0)
+            pl.when(sends_behind)(behind_copy(chunk).start)
         for strip in range(4):
             standardize(strip)
-        for chunks in ((1,), (2, 3)):
-            cols = slice(chunks[0] * 128, chunks[-1] * 128 + 128)
-            ordered[:, cols] = jnp.dot(
-                blocks[1], picks[:, cols], preferred_element_type=F32
-            ).astype(BF16)
-            for chunk in chunks:
-                behind_copy(chunk).start()
-            if CROSS == 0 and chunks[0] == 1:
-                swap(1).start()
+        if CROSS == 0:
+            swap(1).start()
 
     with jax.named_scope("standardize"):
         pl.when(core == 0)(first_core_sends)
@@ -524,13 +567,17 @@
 
     def late_gram(chunk):
         if chunk == 0:
-            raw_standardize(0)
-            raw_standardize(1)
+            pl.when(has_after)(lambda: raw_standardize(0))
+            pl.when(has_before)(lambda: raw_standardize(1))
         else:
             with jax.named_scope("ahead_wait"):
-                arrived(ahead.at[chunk], x_recv.at[0, chunk - 1])
+                pl.when(has_after)(
+                    lambda: arrived(ahead.at[chunk], x_recv.at[0, chunk - 1])
+                )
             with jax.named_scope("behind_wait"):
-                arrived(behind.at[chunk], x_recv.at[1, chunk - 1])
+                pl.when(has_before)(
+                    lambda: arrived(behind.at[chunk], x_recv.at[1, chunk - 1])
+                )
         with jax.named_scope("late_gram"):
             part = part_l.at[chunk]
             for block in range(2):
@@ -548,7 +595,6 @@
             own_term(chunk, 2).start()
 
     scale = 1.0 / samples
-    last = chip == chips - 1
 
     def early_copy():
         return remote(give_e, take_e, f_send.at[0], f_recv.at[0], other)
@@ -569,7 +615,7 @@
             line = slice(first, first + high)
             total = landed(unit, 1) + part_l[chunk, me, line, 128:256]
             cols = slice(512 + 128 * chunk, 640 + 128 * chunk)
-            out[line, cols] = jnp.where(last, 0.0, total * scale)
+            out[line, cols] = total * scale
 
     def end_first(unit):
         chunk, first, high, _ = LATE[unit]
@@ -578,7 +624,7 @@
             arrived(home_l.at[chunk, :, pl.ds(0, 128)], h_recv.at[chunk])
         total = landed(unit, 0) + decode(home_l[chunk, line, 0:128])
         cols = slice(1024 + 128 * chunk, 1152 + 128 * chunk)
-        out[line, cols] = jnp.where(last, 0.0, total * scale)
+        out[line, cols] = total * scale
 
     def end_second(unit):
         chunk, first, high, _ = LATE[unit]
@@ -586,7 +632,7 @@
         if unit == 0 or LATE[unit - 1][0] != chunk:
             arrived(home_l.at[chunk, :, pl.ds(256, 128)], h_recv.at[chunk])
         total = landed(unit, 2) + decode(home_l[chunk, line, 256:384])
-        value = jnp.where(last, 0.0, total * scale)
+        value = total * scale
         for piece in range(high // 8):
             cols = 1024 + 128 * (first // 8 + piece)
             out[8 * chunk : 8 * chunk + 8, cols : cols + 128] = value[
@@ -617,6 +663,11 @@
                 else:
                     end(number)
 
+    def exchange_sent(side):
+        arrived(ahead.at[pl.ds(0, 3)], x_send)
+        for number in range(2):
+            raw_copy(side, number).wait_send()
+
     def first_core():
         run(0)
         with jax.named_scope("ends"):
@@ -628,9 +679,7 @@
         swap(0).wait_send()
         for chain in early[: 2 - CROSS]:
             chain.drain()
-        arrived(ahead.at[pl.ds(0, 3)], x_send)
-        for number in range(2):
-            raw_copy(0, number).wait_send()
+        pl.when(has_before)(lambda: exchange_sent(0))
 
     def second_core():
         run(1)
@@ -645,9 +694,7 @@
             early_copy().wait_send()
         else:
             swap(1).wait_send()
-        arrived(ahead.at[pl.ds(0, 3)], x_send)
-        for number in range(2):
-            raw_copy(1, number).wait_send()
+        pl.when(has_after)(lambda: exchange_sent(1))
         arrived(ours_l.at[:, :, pl.ds(0, 256)], h_send)
 
     pl.when(core == 0)(first_core)
@@ -679,6 +726,7 @@
                 vmem((4, rows, 128), BF16),
                 vmem((4, rows, 128), BF16),
                 vmem((2, rows, 128), BF16),
+                vmem((2, rows, 384), BF16),
                 vmem((2, rows, 128), BF16),
                 vmem((2, rows, 128), BF16),
                 vmem((8, 128), F32),

time: 64.7 us -> 62.8 us (0.971)
  Pallas kernels: 62.9 us -> 61 us
    pallas_call x1, Pallas kernels: 62.9 us -> 61 us  [local(): pl.pallas_call(functools.partial(band_kernel, groups, snps // 2), out_sha...]
where the time goes in v4:
time: 62.8 us; the launch traced here: 62.6 us
  Pallas kernels  61 us (97%)
  local copies, waits for them, and re-layouts  1.62 us (3%)
    pallas_call x1, Pallas kernels, local(): pl.pallas_call(functools.partial(band_kernel, groups, snps // 2), out_sha...  61 us
    unnamed x1, local copies, waits for them, and re-layouts  1.62 us

profile of v4, /device:TPU:1, one launch (start us, length us, event | category | flops | bytes accessed | tf_op | source)
XLA Modules:
  0.0 62.6 jit_solution(4523574656236410424)
XLA Ops:
  0.0 61.0 %band.1 = f32[32,1536]{1,0:T(8,128)} custom-call(bf16[1536,512]{1,0:T(8,128)(2,1)} %dosages.1, s32[1536,512]{1,0:T(8,128)} %observed.1), custom_call_target="tpu_custom_call" | custom-call | flops 2415919104 | bytes 4718592 | tf_op jit(solution)/shard_map/band/pallas_call | solution.py:714
  61.0 1.6 %copy.4 = f32[32,1536]{1,0:T(8,128)} copy(f32[32,1536]{1,0:T(8,128)} %band.1) | data formatting | bytes 393216

commit v5 on v4

--- a/solution.py
+++ b/solution.py
@@ -16,13 +16,13 @@
 FINE = 4096.0
 
 
-OWN_STRIDE = 2
+OWN_STRIDE = 1
 CROSS = 1
 CROSS_STRIDE = 1
 LATE = ((0, 0, 32, 1), (1, 0, 32, 1), (2, 0, 32, 2), (3, 0, 32, 2))
 ORDER = (
-    ((0, 0), (0, 1), (0, 2), (0, 3), (0, 4),),
-    ((0, 0), (1, 0), (2, 0), (3, 0), (1, 1), (0, 1), (2, 1), (4, 0), (3, 1), (1, 2), (2, 2), (0, 2), (5, 0), (3, 2), (2, 3), (1, 3), (4, 1), (0, 3), (3, 3), (2, 4), (1, 4), (5, 1), (3, 4), (2, 5), (4, 2), (0, 4), (1, 5), (5, 2), (3, 5), (2, 6), (1, 6), (4, 3), (3, 6), (2, 7), (5, 3), (1, 7), (4, 4), (3, 7), (2, 8), (1, 8), (5, 4), (3, 8),),
+    ((0, 0), (0, 1), (0, 2), (0, 3), (0, 4), (0, 5), (0, 6), (0, 7), (0, 8),),
+    ((0, 0), (1, 0), (0, 1), (2, 0), (3, 0), (0, 2), (1, 1), (2, 1), (3, 1), (0, 3), (1, 2), (4, 0), (2, 2), (3, 2), (0, 4), (1, 3), (5, 0), (3, 3), (2, 3), (0, 5), (4, 1), (1, 4), (3, 4), (2, 4), (0, 6), (1, 5), (5, 1), (4, 2), (3, 5), (2, 5), (0, 7), (1, 6), (5, 2), (3, 6), (2, 6), (4, 3), (0, 8), (1, 7), (3, 7), (2, 7), (5, 3), (1, 8), (4, 4), (3, 8), (2, 8), (5, 4),),
 )
 
 

time: 62.8 us -> 62.7 us (level)
  no operation moved by 1% of the time
where the time goes in v5:
time: 62.7 us; the launch traced here: 62.6 us
  Pallas kernels  61 us (97%)
  local copies, waits for them, and re-layouts  1.62 us (3%)
    pallas_call x1, Pallas kernels, local(): pl.pallas_call(functools.partial(band_kernel, groups, snps // 2), out_sha...  61 us
    unnamed x1, local copies, waits for them, and re-layouts  1.62 us

profile of v5, /device:TPU:1, one launch (start us, length us, event | category | flops | bytes accessed | tf_op | source)
XLA Modules:
  0.0 62.6 jit_solution(459849830764792254)
XLA Ops:
  0.0 61.0 %band.1 = f32[32,1536]{1,0:T(8,128)} custom-call(bf16[1536,512]{1,0:T(8,128)(2,1)} %dosages.1, s32[1536,512]{1,0:T(8,128)} %observed.1), custom_call_target="tpu_custom_call" | custom-call | flops 2415919104 | bytes 4718592 | tf_op jit(solution)/shard_map/band/pallas_call | solution.py:714
  61.0 1.6 %copy.4 = f32[32,1536]{1,0:T(8,128)} copy(f32[32,1536]{1,0:T(8,128)} %band.1) | data formatting | bytes 393216
